TPU v7x, 32 devices: a whole 2x2x4 slice. The times are simulated.
32 devices in a mesh: freq: 8 (over y, x, core), beam: 4 (over z).
Axes of the slice: x: 2, y: 2, z: 4, core: 2. Of those that a mesh axis runs over, the one named last changes fastest.
Arguments:
- block_samples: bfloat16 [4, 2048, 256], P('beam', 'freq'), may hold values from -6 to 6
- tail_samples: bfloat16 [4, 2048, 2048], P('beam', 'freq'), may hold values from -6 to 6
- tail_blocks: int32 [4], P('beam'), may hold values from 1 to 16, as said below
- dm_limit: int32 [4], P('beam'), may hold values from 256 to 2048, as said below
Outputs:
- peak_snr: float32 [4, 7, 2048], P('beam', None, 'freq')
- excess_snr: float32 [4, 7, 2048], P('beam', None, 'freq')
Inputs may be any that keep to these rules, and one draw needn't show every extreme that they name: `tail_blocks`: some beam has a full tail in every draw. `dm_limit`: some beam searches all trials in every draw.
All inputs are finite; a program needn't handle non-finite values.
Results may differ from a plain program's by a relative error of at most 0.0003.
Values sent between devices are 32-bit elements; how exact they have to be, the bound alone decides.
A program may use at most 64 MiB of HBM per device.

v0:
```python
import jax
import jax.numpy as jnp
import numpy as np
from jax import lax
from jax.sharding import PartitionSpec as P

WIDTHS = 7


def partner_2(block, axis, stride):
    count = lax.axis_size(axis)
    route = []
    for low in range(count):
        high = low | 1 << stride
        if high != low and high < count:
            route += [(low, high), (high, low)]
    return lax.ppermute(block, axis, route)


def skew_rows(series, step_size, base_shift, pad_width):
    dims_of = series.shape
    rows_count = dims_of[-2]
    length_now = dims_of[-1]
    flattened = series.reshape((-1, rows_count, length_now))
    padded = jnp.pad(flattened, ((0, 0), (0, 0), (pad_width, 0)))
    row_width = length_now + pad_width
    lined_up = padded.reshape((flattened.shape[0], rows_count * row_width))
    lined_up = jnp.pad(lined_up, ((0, 0), (0, pad_width)))
    window = lax.dynamic_slice_in_dim(
        lined_up, pad_width - base_shift, rows_count * (row_width - step_size), axis=1
    )
    moved_rows = window.reshape((flattened.shape[0], rows_count, row_width - step_size))[
        :, :, :length_now
    ]
    return moved_rows.reshape(dims_of)


def tree_section(series, offset, reach_max):
    upper_rows = series[..., 0::2, :, :]
    odd_rows = series[..., 1::2, :, :]
    even_moved = skew_rows(odd_rows, 1, (offset + 1) // 2, reach_max)
    odd_moved = skew_rows(odd_rows, 1, (offset + 2) // 2, reach_max)
    joined_rows = jnp.stack([upper_rows + even_moved, upper_rows + odd_moved], axis=-2)
    dims_of = upper_rows.shape
    return joined_rows.reshape(dims_of[:-2] + (2 * dims_of[-2], dims_of[-1]))


def peak_ratios(series, tail_len):
    searched = series[..., tail_len:]
    average = jnp.mean(searched, axis=-1, keepdims=True)
    deviation = jnp.sqrt(jnp.mean((searched - average) ** 2, axis=-1, keepdims=True) + 1e-05)
    reach_back = 2 ** (WIDTHS - 1)
    boxcar = series[..., tail_len - reach_back :]
    results = []
    for width_bit in range(WIDTHS):
        width_now = 2**width_bit
        if width_bit > 0:
            half_width = width_now // 2
            pad_spec = [(0, 0)] * (series.ndim - 1) + [(half_width, 0)]
            boxcar = boxcar + jnp.pad(boxcar[..., :-half_width], pad_spec)
        ratio = (boxcar[..., reach_back:] - width_now * average) / (
            jnp.sqrt(jnp.float32(width_now)) * deviation
        )
        results.append(jnp.max(ratio, axis=-1))
    return jnp.stack(results, axis=-2)


def local(block_samples, tail_samples, tail_blocks, dm_limit):
    beams_dev, local_chan, block_len = block_samples.shape
    tail_len = tail_samples.shape[2]
    valid_mask = (
        jnp.arange(tail_len, dtype=jnp.int32)[None, None, :]
        >= tail_len - 128 * tail_blocks[:, None, None]
    )
    joined = jnp.concatenate(
        [
            jnp.where(valid_mask, tail_samples.astype(jnp.float32), jnp.float32(0.0)),
            block_samples.astype(jnp.float32),
        ],
        axis=-1,
    )
    series = joined[:, :, None, :]
    while series.shape[1] > 1:
        series = tree_section(series, 0, series.shape[2])
    devices = lax.axis_size("freq")
    position = lax.axis_index("freq")
    level_count = devices.bit_length() - 1
    dm_rows = series[:, 0]
    rank_now = jnp.zeros((), jnp.int32)
    for level_bit in range(level_count):
        group_size = 1 << level_bit
        partner = partner_2(dm_rows, "freq", level_bit)
        side_bit = position // group_size % 2
        rank_now = 2 * rank_now + side_bit
        mine_first = side_bit == 0
        upper_half = jnp.where(mine_first, dm_rows, partner)
        lower_half = jnp.where(mine_first, partner, dm_rows)
        base_shift = (rank_now + 1) // 2
        dm_rows = upper_half + skew_rows(
            lower_half, group_size, base_shift, group_size * local_chan
        )
    scores = peak_ratios(dm_rows, tail_len)
    received = lax.all_to_all(scores[..., None], "freq", split_axis=2, concat_axis=3, tiled=True)
    sources = np.arange(devices)
    reorder = np.zeros(devices, dtype=np.int32)
    for level_bit in range(level_count):
        reorder = reorder + ((sources >> level_bit & 1) << level_count - 1 - level_bit).astype(
            np.int32
        )
    received = jnp.take(received, jnp.asarray(reorder), axis=3)
    scores = received.reshape((beams_dev, WIDTHS, local_chan))
    trial_ids = position * local_chan + jnp.arange(local_chan, dtype=jnp.int32)
    peak_snr = jnp.where(
        trial_ids[None, None, :] < dm_limit[:, None, None], scores, jnp.float32(0.0)
    )
    beam_total = lax.psum(jnp.sum(peak_snr, axis=0), "beam")
    excess_snr = peak_snr - beam_total[None] / (beams_dev * lax.axis_size("beam"))
    return (peak_snr, excess_snr)


def solution(mesh):
    return jax.shard_map(
        local,
        mesh=mesh,
        in_specs=(P("beam", "freq", None), P("beam", "freq", None), P("beam"), P("beam")),
        out_specs=(P("beam", None, "freq"), P("beam", None, "freq")),
        check_vma=False,
    )
```

profile of v0, /device:TPU:0, one launch (start us, length us, event | category | flops | bytes accessed | tf_op | source)
XLA Modules:
  0.0 481.2 jit_solution(647264512423135026)
XLA Ops:
  3.9 2.9 slice.163
  7.3 1.7 pad_bitcast_fusion
  10.6 1.5 fusion.34
  12.1 2.1 maximum_bitcast_fusion.1
  17.9 1.7 fusion.50
  19.6 2.0 reshape.433
  21.6 3.8 reshape.435
  25.4 2.6 fusion.11
  29.8 2.9 slice.168
  34.8 1.7 fusion.52
  36.5 3.2 reshape.440
  39.7 1.9 reshape.442
  44.6 3.0 slice.172
  49.1 1.7 fusion.54
  50.8 3.1 reshape.447
  53.9 1.8 reshape.449
  58.9 2.9 slice.176
  63.1 1.7 fusion.53
  64.8 3.1 reshape.454
  67.9 1.8 reshape.456
  74.2 5.5 %slice.180 = f32[1,4,32,2304]{3,1,2,0:T(4,128)} slice(f32[1,8,32,2304]{3,1,2,0:T(8,128)S(1)} %bitcast.199), slice={[0:1:1], [0:8:2], [0:32:1], [0:2304:1]} | slice | bytes 2359296 | tf_op jit(solution)/shard_map/slice | solution.py:39
  81.4 2.3 fusion.51
  83.7 3.7 reshape.461
  87.5 2.5 reshape.463
  91.6 1.7 fusion.21
  93.9 2.1 slice.185
  96.0 10.6 %slice.184 = f32[1,2,64,2304]{3,1,2,0:T(2,128)} slice(f32[1,4,64,2304]{3,1,2,0:T(4,128)S(1)} %bitcast.201), slice={[0:1:1], [0:4:2], [0:64:1], [0:2304:1]} | slice | bytes 2359296 | tf_op jit(solution)/shard_map/slice | solution.py:39
  108.2 3.8 fusion.49
  112.1 3.9 reshape.468
  116.0 2.7 reshape.470
  120.3 2.1 fusion.17
  125.7 14.8 %slice_reduce_fusion.1 = (f32[311168]{0:T(1024)}, f32[311168]{0:T(1024)}) fusion(f32[1,311296]{1,0:T(1,128)S(1)} %bitcast.186), kind=kLoop, calls=%fused_computation.28 | loop fusion | bytes 4978688 | tf_op jit(solution)/shard_map/dynamic_slice | solution.py:29
  140.5 4.1 reshape.498
  144.6 4.1 reshape.499
  148.7 3.5 fusion.35
  152.2 2.0 pad_maximum_fusion.6
  154.7 4.3 collective-permute-done
  159.0 4.1 broadcast_select_fusion
  163.1 1.7 pad.120
  164.9 28.8 %fusion.2 = f32[655104]{0:T(1024)} fusion(s32[]{:T(128)S(6)} %select_n.127, f32[1,655360]{1,0:T(1,128)S(1)} %bitcast.187), kind=kLoop, calls=%fused_computation.12 | loop fusion | bytes 5241860 | tf_op jit(solution)/shard_map/dynamic_slice | solution.py:29
  193.7 6.5 %reshape.500 = f32[1,256,2559]{2,0,1:T(1,128)} reshape(f32[655104]{0:T(1024)} %fusion.2) | data formatting | bytes 5240832 | tf_op jit(solution)/shard_map/reshape | solution.py:32
  200.2 6.3 %fusion.5 = f32[1,256,2304]{2,0,1:T(1,128)} fusion(f32[1,256,2304]{2,0,1:T(1,128)} %collective-permute-done, pred[]{:T(512)S(6)} %eq.15, f32[1,256,2559]{2,0,1:T(1,128)} %reshape.500, f32[1,1,128,2,2304]{4,1,3,2,0:T(1,128)S(1)} %pad_maximum_fusion.6), kind=kLoop, calls=%fused_computation.15 | loop fusion | flops 1179648 | bytes 9437185 | tf_op jit(solution)/shard_map/add | solution.py:99
  206.5 2.9 collective-permute-start.1
  209.4 51.0 %collective-permute-done.1 = f32[1,256,2304]{2,0,1:T(1,128)S(1)} collective-permute-done((f32[1,256,2304]{2,0,1:T(1,128)}, f32[1,256,2304]{2,0,1:T(1,128)S(1)}, u32[]{:S(2)}, u32[]{:S(2)}) %collective-permute-start.1) | collective-permute-done | bytes 2359328 | tf_op jit(solution)/shard_map/ppermute | solution.py:17
  261.9 1.9 pad.122
  263.8 30.2 %fusion.1 = f32[720384]{0:T(1024)S(1)} fusion(s32[]{:T(128)S(6)} %select_n.131, f32[1,720896]{1,0:T(1,128)S(1)} %bitcast.185), kind=kLoop, calls=%fused_computation.10 | loop fusion | bytes 5765124 | tf_op jit(solution)/shard_map/dynamic_slice | solution.py:29
  294.0 5.9 %reshape.501 = f32[1,256,2814]{2,0,1:T(1,128)} reshape(f32[720384]{0:T(1024)S(1)} %fusion.1) | data formatting | bytes 5763072 | tf_op jit(solution)/shard_map/reshape | solution.py:32
  299.9 5.6 %fusion.4 = f32[1,256,2304]{2,0,1:T(1,128)S(1)} fusion(f32[1,256,2304]{2,0,1:T(1,128)} %fusion.5, f32[1,256,2304]{2,0,1:T(1,128)} %copy-done, pred[]{:T(512)S(6)} %eq.14, f32[1,256,2814]{2,0,1:T(1,128)} %reshape.501), kind=kLoop, calls=%fused_computation.14 | loop fusion | flops 1179648 | bytes 9437185 | tf_op jit(solution)/shard_map/add | solution.py:99
  305.6 1.8 collective-permute-start.2
  308.1 49.6 %collective-permute-done.2 = f32[1,256,2304]{2,0,1:T(1,128)} collective-permute-done((f32[1,256,2304]{2,0,1:T(1,128)S(1)}, f32[1,256,2304]{2,0,1:T(1,128)}, u32[]{:S(2)}, u32[]{:S(2)}) %collective-permute-start.2) | collective-permute-done | bytes 2359328 | tf_op jit(solution)/shard_map/ppermute | solution.py:17
  357.7 1.9 broadcast_select_fusion.4
  359.6 2.2 pad.124
  361.8 37.7 %fusion = f32[850944]{0:T(1024)} fusion(s32[]{:T(128)S(6)} %select_n.135, f32[1,851968]{1,0:T(1,128)S(1)} %bitcast.184), kind=kLoop, calls=%fused_computation.8 | loop fusion | bytes 6811652 | tf_op jit(solution)/shard_map/dynamic_slice | solution.py:29
  399.4 9.4 %reshape.502 = f32[1,256,3324]{2,0,1:T(1,128)} reshape(f32[850944]{0:T(1024)} %fusion) | data formatting | bytes 6807552 | tf_op jit(solution)/shard_map/reshape | solution.py:32
  408.8 4.9 %fusion.3 = f32[1,256,2304]{2,0,1:T(1,128)S(1)} fusion(f32[1,256,2304]{2,0,1:T(1,128)S(1)} %fusion.4, f32[1,256,2304]{2,0,1:T(1,128)} %collective-permute-done.2, pred[]{:T(512)S(6)} %eq.13, f32[1,256,3324]{2,0,1:T(1,128)} %reshape.502), kind=kLoop, calls=%fused_computation.13 | loop fusion | flops 1179648 | bytes 9437185 | tf_op jit(solution)/shard_map/add | solution.py:99
  415.6 1.9 slice_add_fusion
  421.0 3.6 multiply_reduce_fusion
  424.6 3.5 divide_reduce_fusion
  428.1 8.7 %fusion.46 = (f32[256]{0:T(256)S(1)}, f32[256]{0:T(256)S(1)}) fusion(f32[1,256,320]{2,0,1:T(1,128)S(1)} %pad_add_fusion.2, f32[256]{0:T(256)S(1)} %get-tuple-element.62, f32[256]{0:T(256)S(1)} %get-tuple-element.55, f32[256]{0:T(256)S(1)} %get-tuple-element.63, f32[256]{0:T(256)S(1)} %get-tuple-element.54, f32[1,256,320]{2,0,1:T(1,128)S(1)} %pad_add_fusion.1), kind=kLoop, calls=%fused_computation.99 | loop fusion | flops 392704 | bytes 530432 | tf_op jit(solution)/shard_map/reduce_max | solution.py:64
  436.9 8.8 %fusion.44 = (f32[256]{0:T(256)S(1)}, f32[256]{0:T(256)S(1)}) fusion(f32[1,256,320]{2,0,1:T(1,128)S(1)} %slice_add_fusion, f32[256]{0:T(256)S(1)} %get-tuple-element.60, f32[256]{0:T(256)S(1)} %get-tuple-element.57, f32[256]{0:T(256)S(1)} %get-tuple-element.61, f32[256]{0:T(256)S(1)} %get-tuple-element.56, f32[1,256,320]{2,0,1:T(1,128)S(1)} %pad_add_fusion.3), kind=kLoop, calls=%fused_computation.97 | loop fusion | flops 392704 | bytes 530432 | tf_op jit(solution)/shard_map/reduce_max | solution.py:64
  445.6 8.8 %fusion.48 = (f32[256]{0:T(256)S(1)}, f32[256]{0:T(256)S(1)}) fusion(f32[1,256,288]{2,0,1:T(1,128)S(1)} %bitcast.213, f32[1,256,320]{2,0,1:T(1,128)S(1)} %pad_add_fusion, f32[256]{0:T(256)S(1)} %get-tuple-element.64, f32[256]{0:T(256)S(1)} %get-tuple-element.53, f32[256]{0:T(256)S(1)} %get-tuple-element.59, f32[256]{0:T(256)S(1)} %get-tuple-element.52), kind=kLoop, calls=%fused_computation.102 | loop fusion | flops 458240 | bytes 563200 | tf_op jit(solution)/shard_map/reduce_max | solution.py:64
  456.8 4.1 all-to-all-start
  460.9 4.7 all-to-all-done
  467.5 12.3 %psum.7 = f32[7,256]{1,0:T(8,128)S(1)} all-reduce(f32[7,256]{1,0:T(8,128)S(1)} %broadcast_select_fusion.6), channel_id=1, replica_groups=mesh['freq'=8,'beam'=4] {'beam'}, use_global_device_ids=true, to_apply=%region_9.10 | all-reduce | flops 1792 | bytes 14336 | tf_op jit(solution)/shard_map/psum | solution.py:116
  (114 shorter events, 48.9 us)
Async XLA Ops:
  14.3 1.4 copy-start.1
  21.6 3.8 copy-start.2
  39.7 1.9 copy-start.3
  41.6 1.3 slice-start
  41.6 1.6 slice-start.1
  53.9 1.8 copy-start.4
  55.7 1.3 slice-start.2
  55.7 1.6 slice-start.3
  67.9 1.9 copy-start.5
  69.8 1.3 slice-start.4
  69.8 1.6 slice-start.5
  87.5 2.5 copy-start.6
  89.9 1.3 slice-start.6
  89.9 1.6 slice-start.7
  116.0 2.7 copy-start.7
  118.7 1.3 slice-start.8
  118.7 1.6 slice-start.9
  154.2 4.8 collective-permute-start
  206.5 53.9 %collective-permute-start.1 = (f32[1,256,2304]{2,0,1:T(1,128)}, f32[1,256,2304]{2,0,1:T(1,128)S(1)}, u32[]{:S(2)}, u32[]{:S(2)}) collective-permute-start(f32[1,256,2304]{2,0,1:T(1,128)} %fusion.5), channel_id=1, source_target_pairs={{0,8},{8,0},{4,12},{12,4},{16,24},{24,16},{20,28},{28,20},{1,9},{9... | collective-permute-start | bytes 7077896 | tf_op jit(solution)/shard_map/ppermute | solution.py:17
  260.4 1.4 copy-start
  299.9 8.1 %copy-start.8 = (s32[8]{0:T(128)S(1)}, s32[8]{0:T(128)}, u32[]{:S(2)}) copy-start(s32[8]{0:T(128)} %constant.210) | copy-start | bytes 100
  305.6 52.1 %collective-permute-start.2 = (f32[1,256,2304]{2,0,1:T(1,128)S(1)}, f32[1,256,2304]{2,0,1:T(1,128)}, u32[]{:S(2)}, u32[]{:S(2)}) collective-permute-start(f32[1,256,2304]{2,0,1:T(1,128)S(1)} %fusion.4), channel_id=1, source_target_pairs={{0,16},{16,0},{4,20},{20,4},{8,24},{24,8},{12,28},{28,12},{1,17},{... | collective-permute-start | bytes 7077896 | tf_op jit(solution)/shard_map/ppermute | solution.py:17
  456.8 8.8 %all-to-all-start = ((f32[8,1,224]{2,1,0:T(1,128)}), f32[8,1,224]{2,1,0:T(1,128)S(1)}, u32[]{:S(2)}, u32[]{:S(2)}) async-start(f32[8,1,224]{2,1,0:T(1,128)} %reshape.514), calls=%async_computation | async-start | bytes 16384 | tf_op jit(solution)/shard_map/all_to_all | solution.py:103
where the time goes:
time: 490 us; the launch traced here: 481 us
  local copies, waits for them, and re-layouts  258 us (53%)
  waiting for transfers between devices  110 us (22%)
  other arithmetic  88.8 us (18%)
  blocking collectives  12.3 us (3%)
  starting transfers between devices  9.28 us (2%)
    dynamic_slice x11, local copies, waits for them, and re-layouts, skew_rows(): lax.dynamic_slice_in_dim(lined_up, pad_width - base_shift, rows_count * (...  125 us
    ppermute x3, waiting for transfers between devices, partner_2(): return lax.ppermute(block, axis, route)  105 us
    reshape x17, local copies, waits for them, and re-layouts, skew_rows(): window.reshape((flattened.shape[0], rows_count, row_width - step_size))  63.4 us
    reduce_max x4, other arithmetic, peak_ratios(): results.append(jnp.max(ratio, axis=-1))  29.8 us
    slice x6, local copies, waits for them, and re-layouts, tree_section(): upper_rows = series[..., 0::2, :, :]  25.5 us
    another operation x16, other arithmetic, tree_section(): jnp.stack([upper_rows + even_moved, upper_rows + odd_moved], axis=-2)  19.6 us
    add x3, other arithmetic, local(): upper_half + skew_rows(lower_half, group_size, base_shift, group_size * l...  16.9 us
    psum x1, blocking collectives, local(): beam_total = lax.psum(jnp.sum(peak_snr, axis=0), 'beam')  12.3 us
  transfers between devices with their start and end apart: 4, of which 4 were waited for; matrix products, arithmetic and copies ran while one was open for 0% of the time, Pallas kernels for 0%

commit v1 on v0

--- a/solution.py
+++ b/solution.py
@@ -1,7 +1,11 @@
+import functools
+
 import jax
 import jax.numpy as jnp
 import numpy as np
 from jax import lax
+from jax.experimental import pallas as pl
+from jax.experimental.pallas import tpu as pltpu
 from jax.sharding import PartitionSpec as P
 
 WIDTHS = 7
@@ -118,9 +122,335 @@
     return (peak_snr, excess_snr)
 
 
+LANES = 128
+MESH_ID = pl.DeviceIdType.MESH
+
+
+def windows(total_levels, keep, span):
+    return [
+        min(-(-(keep + 2 ** (total_levels - s) - 1) // LANES), span + 1)
+        for s in range(total_levels + 1)
+    ]
+
+
+def late_tiles(later, earlier, amount):
+    lane = lax.broadcasted_iota(jnp.int32, (8, LANES), 1)
+    return jnp.where(lane < amount, earlier, later)
+
+
+def shift_uniform(tiles, amount):
+    rolled = [pltpu.roll(x, amount, 1) for x in tiles]
+    lane = lax.broadcasted_iota(jnp.int32, (8, LANES), 1)
+    head = lane < amount
+    return [
+        jnp.where(head, rolled[max(i - 1, 0)], rolled[i]) for i in range(len(tiles))
+    ]
+
+
+def merge_uniform(first, second, amount):
+    even = [a + b for a, b in zip(first, second)]
+    if isinstance(amount, int) and amount == 0:
+        late_first = first
+    else:
+        late_first = shift_uniform(first, amount)
+    late_second = shift_uniform(second, amount + 1)
+    odd = [a + b for a, b in zip(late_first, late_second)]
+    return even, odd
+
+
+def fused(
+    levels,
+    cross,
+    devices,
+    beams,
+    win,
+    tail_tiles,
+    block_tiles,
+    tb_ref,
+    lim_ref,
+    block_ref,
+    tail_ref,
+    peak_ref,
+    excess_ref,
+    split_ref,
+    *rest,
+):
+    stage_refs = rest[: levels - 4]
+    turn_ref, send_ref, recv_ref, snr_ref, beam_ref = rest[levels - 4 : levels + 1]
+    send_sem, recv_sem, bsend_sem, brecv_sem = rest[levels + 1 :]
+    me = lax.axis_index("freq")
+    my_beam = lax.axis_index("beam")
+    chan = 1 << levels
+    half = chan // 2
+    rows = chan // devices
+
+    barrier = pltpu.get_barrier_semaphore()
+    for o in range(1, devices):
+        pl.semaphore_signal(
+            barrier, inc=1, device_id={"freq": lax.rem(me + o, devices)}, device_id_type=MESH_ID
+        )
+    for o in range(1, beams):
+        pl.semaphore_signal(
+            barrier, inc=1, device_id={"beam": lax.rem(my_beam + o, beams)}, device_id_type=MESH_ID
+        )
+
+    groups = half // 8
+    row = lax.broadcasted_iota(jnp.int32, (chan, chan), 0)
+    col = lax.broadcasted_iota(jnp.int32, (chan, chan), 1)
+    inner = row % half
+    wanted = 2 * ((inner % 8) * groups + inner // 8) + row // half
+    pick = jnp.where(col == wanted, 1.0, 0.0).astype(jnp.bfloat16)
+    first_valid = tail_tiles - tb_ref[0]
+    split_ref[0] = jnp.zeros((chan, LANES), jnp.float32)
+    for w in range(0, tail_tiles, 2):
+        part = jnp.dot(
+            pick, tail_ref[0, :, LANES * w : LANES * (w + 2)], preferred_element_type=jnp.float32
+        )
+        for i in range(2):
+            gain = jnp.where(w + i >= first_valid, 1.0, 0.0).astype(jnp.float32)
+            split_ref[1 + w + i] = part[:, LANES * i : LANES * (i + 1)] * gain
+    for w in range(0, block_tiles, 2):
+        part = jnp.dot(
+            pick, block_ref[0, :, LANES * w : LANES * (w + 2)], preferred_element_type=jnp.float32
+        )
+        for i in range(2):
+            split_ref[1 + tail_tiles + w + i] = part[:, LANES * i : LANES * (i + 1)]
+
+    lane_row = lax.broadcasted_iota(jnp.int32, (8, LANES), 0)
+
+    def delayed(load_first, load_second, base, stride, out_tiles, in_tiles):
+        whole = base // LANES
+        short = base % LANES
+        start = in_tiles - out_tiles - whole - 1
+        first, second = load_first(start, out_tiles + 1), load_second(start, out_tiles + 1)
+        dims = first.shape
+        flat = (dims[0] * dims[1], 8, LANES)
+        turned = pltpu.roll(second.reshape(flat), 1, 2).reshape(dims)
+        earlier = jnp.concatenate([turned[:, :1], turned[:, :-1]], axis=1)
+        both = first + late_tiles(turned, earlier, 1)
+        rolled = pltpu.roll(both.reshape(flat), short, 2)
+        rolled = pltpu.roll(rolled, 0, 2, stride=stride, stride_axis=1).reshape(dims)
+        return late_tiles(rolled[:, 1:], rolled[:, :-1], short + stride * lane_row)
+
+    for s in range(levels - 3):
+        out_groups = 1 << (levels - 4 - s)
+        in_tiles, out_tiles = win[s], win[s + 1]
+        low = in_tiles - out_tiles
+        unit = 1 << (levels - 1 - s)
+        trials = 1 << s
+
+        def level_group(g, _, s=s, in_tiles=in_tiles, out_tiles=out_tiles, low=low, unit=unit,
+                        out_groups=out_groups, trials=trials):
+            if s == 0:
+                def load_first(start, count):
+                    return split_ref[pl.ds(start, count), pl.ds(pl.multiple_of(8 * g, 8), 8), :][None]
+
+                def load_second(start, count):
+                    return split_ref[
+                        pl.ds(start, count), pl.ds(pl.multiple_of(half + 8 * g, 8), 8), :
+                    ][None]
+            else:
+                source = stage_refs[s - 1]
+
+                def load_first(start, count):
+                    return source[2 * g, :, pl.ds(start, count)]
+
+                def load_second(start, count):
+                    return source[2 * g + 1, :, pl.ds(start, count)]
+
+            even = load_first(low, out_tiles) + load_second(low, out_tiles)
+            base = me * unit + g
+            odd = delayed(load_first, load_second, base, out_groups, out_tiles, in_tiles)
+            if s + 1 < levels - 3:
+                target = stage_refs[s]
+                for e in range(trials):
+                    target[g, 2 * e] = even[e]
+                    target[g, 2 * e + 1] = odd[e]
+            else:
+                for e in range(trials):
+                    for w in range(out_tiles):
+                        turn_ref[w, 16 * e : 16 * e + 8] = even[e, w]
+                        turn_ref[w, 16 * e + 8 : 16 * e + 16] = odd[e, w]
+            return 0
+
+        if out_groups == 1:
+            level_group(0, 0)
+        else:
+            lax.fori_loop(0, out_groups, level_group, 0)
+
+    pl.semaphore_wait(barrier, devices + beams - 2)
+    tiles = win[levels]
+    per = rows // 8
+    dests = 8 // per
+
+    def last_levels(q, _):
+        nodes = [
+            [
+                [turn_ref[w, pl.ds(64 * q + n, 8, stride=8), :] for w in range(tiles)]
+            ]
+            for n in range(8)
+        ]
+        for s in range(3):
+            merged = []
+            for j in range(len(nodes) // 2):
+                amount = me * (4 >> s) + j
+                grown = []
+                for a, b in zip(nodes[2 * j], nodes[2 * j + 1]):
+                    even, odd = merge_uniform(a, b, amount)
+                    grown += [even, odd]
+                merged.append(grown)
+            nodes = merged
+        for c in range(8):
+            for w in range(tiles):
+                for h in range(dests):
+                    send_ref[dests * q + h, w, pl.ds(c, per, stride=8), :] = nodes[0][c][w][
+                        per * h : per * (h + 1)
+                    ]
+        return 0
+
+    lax.fori_loop(0, chan // 64, last_levels, 0)
+
+    copies = []
+    for o in range(1, devices):
+        target = lax.rem(me + o, devices)
+        copy = pltpu.make_async_remote_copy(
+            src_ref=send_ref.at[target],
+            dst_ref=recv_ref.at[me],
+            send_sem=send_sem.at[o],
+            recv_sem=recv_sem.at[o],
+            device_id={"freq": target},
+            device_id_type=MESH_ID,
+        )
+        copy.start()
+        copies.append(copy)
+    recv_ref[me] = send_ref[me]
+    for copy in copies:
+        copy.wait()
+
+    lane = lax.broadcasted_iota(jnp.int32, (8, LANES), 1)
+    widths = jnp.ones((8, LANES), jnp.float32)
+    roots = jnp.ones((8, LANES), jnp.float32)
+    for i in range(WIDTHS):
+        widths = jnp.where(lane == i, jnp.float32(2**i), widths)
+        roots = jnp.where(lane == i, jnp.sqrt(jnp.float32(2**i)), roots)
+    samples = block_tiles * LANES
+
+    def finish(m, _):
+        nodes = [
+            [
+                [recv_ref[j, w, pl.ds(pl.multiple_of(8 * m, 8), 8), :] for w in range(tiles)]
+            ]
+            for j in range(devices)
+        ]
+        for s in range(cross):
+            merged = []
+            for j in range(len(nodes) // 2):
+                grown = []
+                for a, b in zip(nodes[2 * j], nodes[2 * j + 1]):
+                    even, odd = merge_uniform(a, b, j)
+                    grown += [even, odd]
+                merged.append(grown)
+            nodes = merged
+        for c in range(devices):
+            series = nodes[0][c]
+            block = series[tiles - block_tiles :]
+            average = jnp.sum(sum(block), axis=1, keepdims=True) / samples
+            variance = (
+                jnp.sum(sum((x - average) ** 2 for x in block), axis=1, keepdims=True) / samples
+            )
+            deviation = jnp.sqrt(variance + 1e-05)
+            peaks = jnp.zeros((8, LANES), jnp.float32)
+            box = series
+            for i in range(WIDTHS):
+                if i > 0:
+                    box = [x + y for x, y in zip(box, shift_uniform(box, 2 ** (i - 1)))]
+                top = functools.reduce(jnp.maximum, box[tiles - block_tiles :])
+                peaks = jnp.where(lane == i, jnp.max(top, axis=1, keepdims=True), peaks)
+            ratio = (peaks - widths * average) / (roots * deviation)
+            snr_ref[pl.ds(8 * devices * m + c, 8, stride=devices), :] = ratio
+        return 0
+
+    lax.fori_loop(0, rows // 8, finish, 0)
+
+    peak = snr_ref[...].T[:8]
+    trial = me * chan + lax.broadcasted_iota(jnp.int32, (8, chan), 1)
+    peak = jnp.where(trial < lim_ref[0], peak, 0.0)
+    beam_ref[my_beam] = peak
+    copies = []
+    for o in range(1, beams):
+        copy = pltpu.make_async_remote_copy(
+            src_ref=beam_ref.at[my_beam],
+            dst_ref=beam_ref.at[my_beam],
+            send_sem=bsend_sem.at[o],
+            recv_sem=brecv_sem.at[o],
+            device_id={"beam": lax.rem(my_beam + o, beams)},
+            device_id_type=MESH_ID,
+        )
+        copy.start()
+        copies.append(copy)
+    peak_ref[0] = peak[:WIDTHS]
+    for copy in copies:
+        copy.wait()
+    total = beam_ref[0]
+    for b in range(1, beams):
+        total = total + beam_ref[b]
+    excess_ref[0] = (peak - total / beams)[:WIDTHS]
+
+
+def fused_local(devices, beams, block_samples, tail_samples, tail_blocks, dm_limit):
+    _, chan, block_len = block_samples.shape
+    tail_len = tail_samples.shape[2]
+    levels = chan.bit_length() - 1
+    cross = devices.bit_length() - 1
+    tail_tiles, block_tiles = tail_len // LANES, block_len // LANES
+    win = windows(levels + cross, block_len + 2 ** (WIDTHS - 1) - 1, tail_tiles + block_tiles)
+    rows = chan // devices
+    scratch = [pltpu.VMEM((win[0], chan, LANES), jnp.float32)]
+    for s in range(1, levels - 3):
+        scratch.append(
+            pltpu.VMEM((1 << (levels - 3 - s), 1 << s, win[s], 8, LANES), jnp.float32)
+        )
+    tiles = win[levels]
+    scratch += [
+        pltpu.VMEM((tiles, chan, LANES), jnp.float32),
+        pltpu.VMEM((devices, tiles, rows, LANES), jnp.float32),
+        pltpu.VMEM((devices, tiles, rows, LANES), jnp.float32),
+        pltpu.VMEM((chan, LANES), jnp.float32),
+        pltpu.VMEM((beams, 8, chan), jnp.float32),
+        pltpu.SemaphoreType.DMA((devices,)),
+        pltpu.SemaphoreType.DMA((devices,)),
+        pltpu.SemaphoreType.DMA((beams,)),
+        pltpu.SemaphoreType.DMA((beams,)),
+    ]
+    out = jax.ShapeDtypeStruct((1, WIDTHS, chan), jnp.float32)
+    return pl.pallas_call(
+        functools.partial(fused, levels, cross, devices, beams, win, tail_tiles, block_tiles),
+        out_shape=(out, out),
+        in_specs=[pl.BlockSpec(memory_space=pltpu.SMEM)] * 2
+        + [pl.BlockSpec(memory_space=pltpu.VMEM)] * 2,
+        out_specs=(pl.BlockSpec(memory_space=pltpu.VMEM),) * 2,
+        scratch_shapes=scratch,
+        compiler_params=pltpu.CompilerParams(
+            collective_id=0, has_side_effects=True, vmem_limit_bytes=48 * 2**20
+        ),
+    )(tail_blocks, dm_limit, block_samples, tail_samples)
+
+
+def fits(devices, beams_all, beams, chan):
+    return beams_all == beams and chan % (8 * devices) == 0 and chan <= 64 * devices and chan >= 64
+
+
 def solution(mesh):
+    devices, beams = mesh.shape["freq"], mesh.shape["beam"]
+
+    def body(block_samples, tail_samples, tail_blocks, dm_limit):
+        args = (block_samples, tail_samples, tail_blocks, dm_limit)
+        if fits(devices, beams * block_samples.shape[0], beams, block_samples.shape[1]):
+            return fused_local(devices, beams, *args)
+        return local(*args)
+
     return jax.shard_map(
-        local,
+        body,
         mesh=mesh,
         in_specs=(P("beam", "freq", None), P("beam", "freq", None), P("beam"), P("beam")),
         out_specs=(P("beam", None, "freq"), P("beam", None, "freq")),

time: 490 us -> 36.5 us (0.07); the launches traced: 481 us -> 36.3 us
  local copies, waits for them, and re-layouts: 258 us -> 3.32 us
  waiting for transfers between devices: 110 us -> 0 us
  other arithmetic: 88.8 us -> 0 us
  Pallas kernels: 0 us -> 31.1 us
  blocking collectives: 12.3 us -> 0 us
  starting transfers between devices: 9.28 us -> 0 us
    dynamic_slice x11 -> x0, local copies, waits for them, and re-layouts: 125 us -> none  [skew_rows(): lax.dynamic_slice_in_dim(lined_up, pad_width - base_shift, rows_count * (...]
    ppermute x3 -> x0, waiting for transfers between devices: 105 us -> none  [partner_2(): return lax.ppermute(block, axis, route)]
    reshape x26 -> x0, local copies, waits for them, and re-layouts: 71 us -> none  [the longest x17 63.4 us: skew_rows(): window.reshape((flattened.shape[0], rows_count, row_width - step_size))]
    slice x33 -> x0, local copies, waits for them, and re-layouts: 41.9 us -> none  [the longest x6 25.5 us: tree_section(): upper_rows = series[..., 0::2, :, :]]
    pallas_call x0 -> x1, Pallas kernels: none -> 31.1 us  [fused_local(): pl.pallas_call(functools.partial(fused, levels, cross, devices, beams, wi...]
    reduce_max x4 -> x0, other arithmetic: 29.8 us -> none  [peak_ratios(): results.append(jnp.max(ratio, axis=-1))]
    add x8 -> x0, other arithmetic: 22.2 us -> none  [the longest x3 16.9 us: local(): upper_half + skew_rows(lower_half, group_size, base_shift, group_size * l...]
    another operation x16 -> x0, other arithmetic: 19.6 us -> none  [tree_section(): jnp.stack([upper_rows + even_moved, upper_rows + odd_moved], axis=-2)]
  transfers between devices with their start and end apart: 4 -> 0, of which waited for: 4 -> 0; matrix products, arithmetic and copies ran while one was open for 0% -> 0% of each run, Pallas kernels for 0% -> 0%
where the time goes in v1:
time: 36.5 us; the launch traced here: 36.3 us
  Pallas kernels  31.1 us (85%)
  local copies, waits for them, and re-layouts  3.32 us (9%)
  between operations  1.94 us (5%)
    pallas_call x1, Pallas kernels, fused_local(): pl.pallas_call(functools.partial(fused, levels, cross, devices, beams, wi...  31.1 us
    unnamed x4, local copies, waits for them, and re-layouts  2.12 us
    pallas_call x2, local copies, waits for them, and re-layouts, fused_local(): pl.pallas_call(functools.partial(fused, levels, cross, devices, beams, wi...  1.2 us

profile of v1, /device:TPU:0, one launch (start us, length us, event | category | flops | bytes accessed | tf_op | source)
XLA Modules:
  0.0 36.3 jit_solution(17350457081192878889)
XLA Ops:
  1.9 0.0 copy-start
  1.9 1.2 %copy-done = bf16[1,256,2048]{2,1,0:T(8,128)(2,1)S(1)} copy-done((bf16[1,256,2048]{2,1,0:T(8,128)(2,1)S(1)}, bf16[1,256,2048]{2,1,0:T(8,128)(2,1)}, u32[]{:S(2)}) %copy-start) | copy-done | bytes 1048600
  3.1 0.0 copy-start.1
  3.1 0.9 %copy-done.1 = bf16[1,256,256]{2,1,0:T(8,128)(2,1)S(1)} copy-done((bf16[1,256,256]{2,1,0:T(8,128)(2,1)S(1)}, bf16[1,256,256]{2,1,0:T(8,128)(2,1)}, u32[]{:S(2)}) %copy-start.1) | copy-done | bytes 131096
  4.1 31.1 %shard_map.59 = (f32[1,7,256]{2,1,0:T(8,128)S(1)}, f32[1,7,256]{2,1,0:T(8,128)S(1)}) custom-call(s32[1]{0:T(128)S(6)} %copy.8.tb_ref, s32[1]{0:T(128)S(6)} %copy.9.lim_ref, bf16[1,256,256]{2,1,0:T(8,128)(2,1)S(1)} %copy-done.1, bf16[1,256,2048]{2,1,0:T(8,128)(2,1)S(1)} %copy-done), custom_call_target="tpu_custom_call" | custom-call | tf_op jit(solution)/shard_map/pallas_call | solution.py:426
  35.1 0.6 %copy.6 = f32[1,7,256]{2,0,1:T(1,128)} copy(f32[1,7,256]{2,1,0:T(8,128)S(1)} %get-tuple-element.2) | data formatting | bytes 14336 | tf_op jit(solution)/shard_map/pallas_call | solution.py:426
  35.7 0.6 %copy.7 = f32[1,7,256]{2,0,1:T(1,128)} copy(f32[1,7,256]{2,1,0:T(8,128)S(1)} %get-tuple-element.3) | data formatting | bytes 14336 | tf_op jit(solution)/shard_map/pallas_call | solution.py:426
Async XLA Ops:
  1.9 1.2 %copy-start = (bf16[1,256,2048]{2,1,0:T(8,128)(2,1)S(1)}, bf16[1,256,2048]{2,1,0:T(8,128)(2,1)}, u32[]{:S(2)}) copy-start(bf16[1,256,2048]{2,1,0:T(8,128)(2,1)} %tail_ref.1) | copy-start | bytes 3145732
  3.1 0.9 %copy-start.1 = (bf16[1,256,256]{2,1,0:T(8,128)(2,1)S(1)}, bf16[1,256,256]{2,1,0:T(8,128)(2,1)}, u32[]{:S(2)}) copy-start(bf16[1,256,256]{2,1,0:T(8,128)(2,1)} %block_ref.1) | copy-start | bytes 393220

commit v2 on v1

--- a/solution.py
+++ b/solution.py
@@ -123,6 +123,8 @@
 
 
 LANES = 128
+PIECE = 512
+UNROLL = 4
 MESH_ID = pl.DeviceIdType.MESH
 
 
@@ -176,13 +178,23 @@
     *rest,
 ):
     stage_refs = rest[: levels - 4]
-    turn_ref, send_ref, recv_ref, snr_ref, beam_ref = rest[levels - 4 : levels + 1]
-    send_sem, recv_sem, bsend_sem, brecv_sem = rest[levels + 1 :]
+    turn_ref, send_ref, recv_ref, snr_ref, beam_ref, held_ref = rest[levels - 4 : levels + 2]
+    load_sem, send_sem, recv_sem, bsend_sem, brecv_sem = rest[levels + 2 :]
     me = lax.axis_index("freq")
     my_beam = lax.axis_index("beam")
     chan = 1 << levels
     half = chan // 2
     rows = chan // devices
+    tail_len, block_len = tail_tiles * LANES, block_tiles * LANES
+    pieces = [(tail_ref, at, at, PIECE) for at in range(0, tail_len, PIECE)]
+    pieces.append((block_ref, 0, tail_len, block_len))
+    loads = []
+    for i, (source, at, to, size) in enumerate(pieces):
+        load = pltpu.make_async_copy(
+            source.at[0, :, at : at + size], held_ref.at[:, to : to + size], load_sem.at[i]
+        )
+        load.start()
+        loads.append(load)
 
     barrier = pltpu.get_barrier_semaphore()
     for o in range(1, devices):
@@ -202,19 +214,17 @@
     pick = jnp.where(col == wanted, 1.0, 0.0).astype(jnp.bfloat16)
     first_valid = tail_tiles - tb_ref[0]
     split_ref[0] = jnp.zeros((chan, LANES), jnp.float32)
-    for w in range(0, tail_tiles, 2):
-        part = jnp.dot(
-            pick, tail_ref[0, :, LANES * w : LANES * (w + 2)], preferred_element_type=jnp.float32
-        )
-        for i in range(2):
-            gain = jnp.where(w + i >= first_valid, 1.0, 0.0).astype(jnp.float32)
-            split_ref[1 + w + i] = part[:, LANES * i : LANES * (i + 1)] * gain
-    for w in range(0, block_tiles, 2):
-        part = jnp.dot(
-            pick, block_ref[0, :, LANES * w : LANES * (w + 2)], preferred_element_type=jnp.float32
-        )
-        for i in range(2):
-            split_ref[1 + tail_tiles + w + i] = part[:, LANES * i : LANES * (i + 1)]
+    for i, (_, _, to, size) in enumerate(pieces):
+        loads[i].wait()
+        for w in range(to // LANES, (to + size) // LANES, 2):
+            part = jnp.dot(
+                pick, held_ref[:, LANES * w : LANES * (w + 2)], preferred_element_type=jnp.float32
+            )
+            for k in range(2):
+                tile = part[:, LANES * k : LANES * (k + 1)]
+                if w < tail_tiles:
+                    tile = tile * jnp.where(w + k >= first_valid, 1.0, 0.0).astype(jnp.float32)
+                split_ref[1 + w + k] = tile
 
     lane_row = lax.broadcasted_iota(jnp.int32, (8, LANES), 0)
 
@@ -223,14 +233,12 @@
         short = base % LANES
         start = in_tiles - out_tiles - whole - 1
         first, second = load_first(start, out_tiles + 1), load_second(start, out_tiles + 1)
-        dims = first.shape
-        flat = (dims[0] * dims[1], 8, LANES)
-        turned = pltpu.roll(second.reshape(flat), 1, 2).reshape(dims)
-        earlier = jnp.concatenate([turned[:, :1], turned[:, :-1]], axis=1)
+        turned = pltpu.roll(second, 1, 2)
+        earlier = jnp.concatenate([turned[:1], turned[:-1]], axis=0)
         both = first + late_tiles(turned, earlier, 1)
-        rolled = pltpu.roll(both.reshape(flat), short, 2)
-        rolled = pltpu.roll(rolled, 0, 2, stride=stride, stride_axis=1).reshape(dims)
-        return late_tiles(rolled[:, 1:], rolled[:, :-1], short + stride * lane_row)
+        rolled = pltpu.roll(both, short, 2)
+        rolled = pltpu.roll(rolled, 0, 2, stride=stride, stride_axis=1)
+        return late_tiles(rolled[1:], rolled[:-1], short + stride * lane_row)
 
     for s in range(levels - 3):
         out_groups = 1 << (levels - 4 - s)
@@ -239,54 +247,60 @@
         unit = 1 << (levels - 1 - s)
         trials = 1 << s
 
-        def level_group(g, _, s=s, in_tiles=in_tiles, out_tiles=out_tiles, low=low, unit=unit,
-                        out_groups=out_groups, trials=trials):
+        def level_group(g, e, s=s, in_tiles=in_tiles, out_tiles=out_tiles, low=low, unit=unit,
+                        out_groups=out_groups):
             if s == 0:
                 def load_first(start, count):
-                    return split_ref[pl.ds(start, count), pl.ds(pl.multiple_of(8 * g, 8), 8), :][None]
+                    return split_ref[pl.ds(start, count), pl.ds(pl.multiple_of(8 * g, 8), 8), :]
 
                 def load_second(start, count):
                     return split_ref[
                         pl.ds(start, count), pl.ds(pl.multiple_of(half + 8 * g, 8), 8), :
-                    ][None]
+                    ]
             else:
                 source = stage_refs[s - 1]
 
                 def load_first(start, count):
-                    return source[2 * g, :, pl.ds(start, count)]
+                    return source[2 * g, e, pl.ds(start, count)]
 
                 def load_second(start, count):
-                    return source[2 * g + 1, :, pl.ds(start, count)]
+                    return source[2 * g + 1, e, pl.ds(start, count)]
 
             even = load_first(low, out_tiles) + load_second(low, out_tiles)
-            base = me * unit + g
-            odd = delayed(load_first, load_second, base, out_groups, out_tiles, in_tiles)
+            odd = delayed(load_first, load_second, me * unit + g, out_groups, out_tiles, in_tiles)
             if s + 1 < levels - 3:
                 target = stage_refs[s]
+                target[g, 2 * e] = even
+                target[g, 2 * e + 1] = odd
+            else:
+                for w in range(out_tiles):
+                    turn_ref[w, 16 * e : 16 * e + 8] = even[w]
+                    turn_ref[w, 16 * e + 8 : 16 * e + 16] = odd[w]
+
+        at_once = min(out_groups, UNROLL)
+
+        def level_groups(i, _, level_group=level_group, at_once=at_once, trials=trials):
+            for k in range(at_once):
                 for e in range(trials):
-                    target[g, 2 * e] = even[e]
-                    target[g, 2 * e + 1] = odd[e]
-            else:
-                for e in range(trials):
-                    for w in range(out_tiles):
-                        turn_ref[w, 16 * e : 16 * e + 8] = even[e, w]
-                        turn_ref[w, 16 * e + 8 : 16 * e + 16] = odd[e, w]
+                    level_group(at_once * i + k, e)
             return 0
 
-        if out_groups == 1:
-            level_group(0, 0)
+        if out_groups == at_once:
+            level_groups(0, 0)
         else:
-            lax.fori_loop(0, out_groups, level_group, 0)
+            lax.fori_loop(0, out_groups // at_once, level_groups, 0)
 
     pl.semaphore_wait(barrier, devices + beams - 2)
     tiles = win[levels]
     per = rows // 8
     dests = 8 // per
 
-    def last_levels(q, _):
+    def last_levels(q):
         nodes = [
             [
-                [turn_ref[w, pl.ds(64 * q + n, 8, stride=8), :] for w in range(tiles)]
+                [turn_ref[w, pl.ds(pl.multiple_of(64 * q, 64) + n, 8, stride=8), :]
+                    for w in range(tiles)
+                ]
             ]
             for n in range(8)
         ]
@@ -306,26 +320,32 @@
                     send_ref[dests * q + h, w, pl.ds(c, per, stride=8), :] = nodes[0][c][w][
                         per * h : per * (h + 1)
                     ]
-        return 0
-
-    lax.fori_loop(0, chan // 64, last_levels, 0)
-
-    copies = []
-    for o in range(1, devices):
-        target = lax.rem(me + o, devices)
-        copy = pltpu.make_async_remote_copy(
+
+    def exchange(target, source):
+        return pltpu.make_async_remote_copy(
             src_ref=send_ref.at[target],
-            dst_ref=recv_ref.at[me],
-            send_sem=send_sem.at[o],
-            recv_sem=recv_sem.at[o],
+            dst_ref=recv_ref.at[source],
+            send_sem=send_sem.at[target],
+            recv_sem=recv_sem.at[source],
             device_id={"freq": target},
             device_id_type=MESH_ID,
         )
-        copy.start()
-        copies.append(copy)
+
+    chunks = chan // 64
+    own = me // dests
+    for i in range(1, chunks):
+        q = lax.rem(own + i, chunks)
+        last_levels(q)
+        for h in range(dests):
+            exchange(dests * q + h, me).start()
+    last_levels(own)
+    for h in range(1, dests):
+        exchange(dests * own + lax.rem(me + h, dests), me).start()
     recv_ref[me] = send_ref[me]
-    for copy in copies:
-        copy.wait()
+    for o in range(1, devices):
+        other = lax.rem(me + o, devices)
+        exchange(other, me).wait_send()
+        exchange(other, other).wait_recv()
 
     lane = lax.broadcasted_iota(jnp.int32, (8, LANES), 1)
     widths = jnp.ones((8, LANES), jnp.float32)
@@ -335,7 +355,7 @@
         roots = jnp.where(lane == i, jnp.sqrt(jnp.float32(2**i)), roots)
     samples = block_tiles * LANES
 
-    def finish(m, _):
+    def finish(m):
         nodes = [
             [
                 [recv_ref[j, w, pl.ds(pl.multiple_of(8 * m, 8), 8), :] for w in range(tiles)]
@@ -368,9 +388,13 @@
                 peaks = jnp.where(lane == i, jnp.max(top, axis=1, keepdims=True), peaks)
             ratio = (peaks - widths * average) / (roots * deviation)
             snr_ref[pl.ds(8 * devices * m + c, 8, stride=devices), :] = ratio
+
+    def finish_both(i, _):
+        finish(2 * i)
+        finish(2 * i + 1)
         return 0
 
-    lax.fori_loop(0, rows // 8, finish, 0)
+    lax.fori_loop(0, rows // 16, finish_both, 0)
 
     peak = snr_ref[...].T[:8]
     trial = me * chan + lax.broadcasted_iota(jnp.int32, (8, chan), 1)
@@ -417,6 +441,8 @@
         pltpu.VMEM((devices, tiles, rows, LANES), jnp.float32),
         pltpu.VMEM((chan, LANES), jnp.float32),
         pltpu.VMEM((beams, 8, chan), jnp.float32),
+        pltpu.VMEM((chan, tail_len + block_len), jnp.bfloat16),
+        pltpu.SemaphoreType.DMA((tail_len // PIECE + 1,)),
         pltpu.SemaphoreType.DMA((devices,)),
         pltpu.SemaphoreType.DMA((devices,)),
         pltpu.SemaphoreType.DMA((beams,)),
@@ -427,7 +453,7 @@
         functools.partial(fused, levels, cross, devices, beams, win, tail_tiles, block_tiles),
         out_shape=(out, out),
         in_specs=[pl.BlockSpec(memory_space=pltpu.SMEM)] * 2
-        + [pl.BlockSpec(memory_space=pltpu.VMEM)] * 2,
+        + [pl.BlockSpec(memory_space=pltpu.HBM)] * 2,
         out_specs=(pl.BlockSpec(memory_space=pltpu.VMEM),) * 2,
         scratch_shapes=scratch,
         compiler_params=pltpu.CompilerParams(
@@ -437,7 +463,7 @@
 
 
 def fits(devices, beams_all, beams, chan):
-    return beams_all == beams and chan % (8 * devices) == 0 and chan <= 64 * devices and chan >= 64
+    return beams_all == beams and chan % (16 * devices) == 0 and chan <= 64 * devices and chan >= 64
 
 
 def solution(mesh):

time: 36.5 us -> 40 us (1.096)
  Pallas kernels: 31.1 us -> 34.5 us
    pallas_call x1, Pallas kernels: 31.1 us -> 34.5 us  [fused_local(): pl.pallas_call(functools.partial(fused, levels, cross, devices, beams, wi...]
where the time goes in v2:
time: 40 us; the launch traced here: 39.8 us
  Pallas kernels  34.5 us (86%)
  local copies, waits for them, and re-layouts  3.32 us (8%)
  between operations  1.94 us (5%)
    pallas_call x1, Pallas kernels, fused_local(): pl.pallas_call(functools.partial(fused, levels, cross, devices, beams, wi...  34.5 us
    unnamed x4, local copies, waits for them, and re-layouts  2.12 us
    pallas_call x2, local copies, waits for them, and re-layouts, fused_local(): pl.pallas_call(functools.partial(fused, levels, cross, devices, beams, wi...  1.2 us

profile of v2, /device:TPU:0, one launch (start us, length us, event | category | flops | bytes accessed | tf_op | source)
XLA Modules:
  0.0 39.8 jit_solution(16134709050052375763)
XLA Ops:
  1.9 0.0 copy-start
  1.9 1.2 %copy-done = bf16[1,256,2048]{2,1,0:T(8,128)(2,1)S(1)} copy-done((bf16[1,256,2048]{2,1,0:T(8,128)(2,1)S(1)}, bf16[1,256,2048]{2,1,0:T(8,128)(2,1)}, u32[]{:S(2)}) %copy-start) | copy-done | bytes 1048600
  3.1 0.0 copy-start.1
  3.1 0.9 %copy-done.1 = bf16[1,256,256]{2,1,0:T(8,128)(2,1)S(1)} copy-done((bf16[1,256,256]{2,1,0:T(8,128)(2,1)S(1)}, bf16[1,256,256]{2,1,0:T(8,128)(2,1)}, u32[]{:S(2)}) %copy-start.1) | copy-done | bytes 131096
  4.1 34.5 %shard_map.59 = (f32[1,7,256]{2,1,0:T(8,128)S(1)}, f32[1,7,256]{2,1,0:T(8,128)S(1)}) custom-call(s32[1]{0:T(128)S(6)} %copy.8.tb_ref, s32[1]{0:T(128)S(6)} %copy.9.lim_ref, bf16[1,256,256]{2,1,0:T(8,128)(2,1)S(1)} %copy-done.1, bf16[1,256,2048]{2,1,0:T(8,128)(2,1)S(1)} %copy-done), custom_call_target="tpu_custom_call" | custom-call | tf_op jit(solution)/shard_map/pallas_call | solution.py:452
  38.6 0.6 %copy.6 = f32[1,7,256]{2,0,1:T(1,128)} copy(f32[1,7,256]{2,1,0:T(8,128)S(1)} %get-tuple-element.2) | data formatting | bytes 14336 | tf_op jit(solution)/shard_map/pallas_call | solution.py:452
  39.2 0.6 %copy.7 = f32[1,7,256]{2,0,1:T(1,128)} copy(f32[1,7,256]{2,1,0:T(8,128)S(1)} %get-tuple-element.3) | data formatting | bytes 14336 | tf_op jit(solution)/shard_map/pallas_call | solution.py:452
Async XLA Ops:
  1.9 1.2 %copy-start = (bf16[1,256,2048]{2,1,0:T(8,128)(2,1)S(1)}, bf16[1,256,2048]{2,1,0:T(8,128)(2,1)}, u32[]{:S(2)}) copy-start(bf16[1,256,2048]{2,1,0:T(8,128)(2,1)} %tail_ref.1) | copy-start | bytes 3145732
  3.1 0.9 %copy-start.1 = (bf16[1,256,256]{2,1,0:T(8,128)(2,1)S(1)}, bf16[1,256,256]{2,1,0:T(8,128)(2,1)}, u32[]{:S(2)}) copy-start(bf16[1,256,256]{2,1,0:T(8,128)(2,1)} %block_ref.1) | copy-start | bytes 393220

commit v3 on v2

--- a/solution.py
+++ b/solution.py
@@ -123,16 +123,26 @@
 
 
 LANES = 128
-PIECE = 512
-UNROLL = 4
+PIECE = 256
+SPLITS = 3
+AT_ONCE = (2, 4, 4, 4, 4)
 MESH_ID = pl.DeviceIdType.MESH
 
 
-def windows(total_levels, keep, span):
-    return [
-        min(-(-(keep + 2 ** (total_levels - s) - 1) // LANES), span + 1)
-        for s in range(total_levels + 1)
-    ]
+def windows(levels, devices, keep):
+    need = [0] * (levels + 1)
+    need[levels] = keep + devices - 1
+    for s in reversed(range(levels)):
+        unit = 1 << (levels - 1 - s)
+        if s >= levels - 3:
+            need[s] = need[s + 1] + devices * unit
+        else:
+            start = need[s + 1]
+            if s == levels - 4:
+                start += 7 * ((1 << (levels - 3)) - 1)
+                need[s + 1] = start
+            need[s] = start + (devices - 1) * unit + unit // 8
+    return [-(-n // LANES) for n in need]
 
 
 def late_tiles(later, earlier, amount):
@@ -187,7 +197,7 @@
     rows = chan // devices
     tail_len, block_len = tail_tiles * LANES, block_tiles * LANES
     pieces = [(tail_ref, at, at, PIECE) for at in range(0, tail_len, PIECE)]
-    pieces.append((block_ref, 0, tail_len, block_len))
+    pieces += [(block_ref, at, tail_len + at, PIECE) for at in range(0, block_len, PIECE)]
     loads = []
     for i, (source, at, to, size) in enumerate(pieces):
         load = pltpu.make_async_copy(
@@ -213,97 +223,104 @@
     wanted = 2 * ((inner % 8) * groups + inner // 8) + row // half
     pick = jnp.where(col == wanted, 1.0, 0.0).astype(jnp.bfloat16)
     first_valid = tail_tiles - tb_ref[0]
-    split_ref[0] = jnp.zeros((chan, LANES), jnp.float32)
-    for i, (_, _, to, size) in enumerate(pieces):
-        loads[i].wait()
-        for w in range(to // LANES, (to + size) // LANES, 2):
-            part = jnp.dot(
-                pick, held_ref[:, LANES * w : LANES * (w + 2)], preferred_element_type=jnp.float32
-            )
-            for k in range(2):
-                tile = part[:, LANES * k : LANES * (k + 1)]
-                if w < tail_tiles:
-                    tile = tile * jnp.where(w + k >= first_valid, 1.0, 0.0).astype(jnp.float32)
-                split_ref[1 + w + k] = tile
-
-    lane_row = lax.broadcasted_iota(jnp.int32, (8, LANES), 0)
-
-    def delayed(load_first, load_second, base, stride, out_tiles, in_tiles):
-        whole = base // LANES
-        short = base % LANES
-        start = in_tiles - out_tiles - whole - 1
-        first, second = load_first(start, out_tiles + 1), load_second(start, out_tiles + 1)
-        turned = pltpu.roll(second, 1, 2)
-        earlier = jnp.concatenate([turned[:1], turned[:-1]], axis=0)
-        both = first + late_tiles(turned, earlier, 1)
-        rolled = pltpu.roll(both, short, 2)
-        rolled = pltpu.roll(rolled, 0, 2, stride=stride, stride_axis=1)
-        return late_tiles(rolled[1:], rolled[:-1], short + stride * lane_row)
-
+    fill = split_ref.shape[0] - tail_tiles - block_tiles
+    split_ref[:fill] = jnp.zeros((fill, chan, LANES), jnp.float32)
+
+    def split(i, _):
+        for k in range(SPLITS):
+            at = pl.multiple_of((SPLITS * i + k) * PIECE, PIECE)
+            piece = held_ref.at[:, pl.ds(at, PIECE)]
+            pltpu.make_async_copy(
+                block_ref.at[0, :, :PIECE], piece, load_sem.at[SPLITS * i + k]
+            ).wait()
+            part = jnp.dot(pick, piece[...], preferred_element_type=jnp.float32)
+            for h in range(PIECE // LANES):
+                tile = (SPLITS * i + k) * (PIECE // LANES) + h
+                gain = jnp.where(tile >= first_valid, 1.0, 0.0).astype(jnp.float32)
+                split_ref[fill + tile] = part[:, LANES * h : LANES * (h + 1)] * gain
+        return 0
+
+    lax.fori_loop(0, len(pieces) // SPLITS, split, 0)
+
+    for ref in stage_refs:
+        ref[:, :, 0] = jnp.zeros((ref.shape[0], ref.shape[1], 8, LANES), jnp.float32)
+    lane_row = lax.broadcasted_iota(jnp.int32, (8, LANES), 1)
     for s in range(levels - 3):
         out_groups = 1 << (levels - 4 - s)
-        in_tiles, out_tiles = win[s], win[s + 1]
-        low = in_tiles - out_tiles
+        out_tiles = win[s + 1]
         unit = 1 << (levels - 1 - s)
         trials = 1 << s
 
-        def level_group(g, e, s=s, in_tiles=in_tiles, out_tiles=out_tiles, low=low, unit=unit,
-                        out_groups=out_groups):
+        def level_pair(index, s=s, out_tiles=out_tiles, unit=unit, trials=trials):
+            g, e = index // trials, index % trials
             if s == 0:
-                def load_first(start, count):
-                    return split_ref[pl.ds(start, count), pl.ds(pl.multiple_of(8 * g, 8), 8), :]
-
-                def load_second(start, count):
-                    return split_ref[
-                        pl.ds(start, count), pl.ds(pl.multiple_of(half + 8 * g, 8), 8), :
-                    ]
+                held_tiles = split_ref.shape[0]
+
+                def load(which, start, count):
+                    at = pl.multiple_of(half * which + 8 * g, 8)
+                    return split_ref[pl.ds(start, count), pl.ds(at, 8), :]
             else:
                 source = stage_refs[s - 1]
-
-                def load_first(start, count):
-                    return source[2 * g, e, pl.ds(start, count)]
-
-                def load_second(start, count):
-                    return source[2 * g + 1, e, pl.ds(start, count)]
-
-            even = load_first(low, out_tiles) + load_second(low, out_tiles)
-            odd = delayed(load_first, load_second, me * unit + g, out_groups, out_tiles, in_tiles)
+                held_tiles = source.shape[2]
+
+                def load(which, start, count):
+                    return source[2 * g + which, e, pl.ds(start, count)]
+
+            low = held_tiles - out_tiles
+            even = load(0, low, out_tiles) + load(1, low, out_tiles)
+            base = me * unit + g
+            start, short = low - base // LANES - 1, base % LANES
+            first = pltpu.roll(load(0, start, out_tiles + 1), short, 2)
+            second = pltpu.roll(load(1, start, out_tiles + 1), short + 1, 2)
+            odd = late_tiles(first[1:], first[:-1], short) + late_tiles(
+                second[1:], second[:-1], short + 1
+            )
             if s + 1 < levels - 3:
                 target = stage_refs[s]
-                target[g, 2 * e] = even
-                target[g, 2 * e + 1] = odd
+                target[g, 2 * e, 1:] = even
+                target[g, 2 * e + 1, 1:] = odd
             else:
-                for w in range(out_tiles):
-                    turn_ref[w, 16 * e : 16 * e + 8] = even[w]
-                    turn_ref[w, 16 * e + 8 : 16 * e + 16] = odd[w]
-
-        at_once = min(out_groups, UNROLL)
-
-        def level_groups(i, _, level_group=level_group, at_once=at_once, trials=trials):
+                at = pl.multiple_of(16 * e, 16)
+                turn_ref[:, pl.ds(at, 8)] = even
+                turn_ref[:, pl.ds(at + 8, 8)] = odd
+
+        at_once = AT_ONCE[min(s, len(AT_ONCE) - 1)]
+
+        def level_pairs(i, _, level_pair=level_pair, at_once=at_once):
             for k in range(at_once):
-                for e in range(trials):
-                    level_group(at_once * i + k, e)
+                level_pair(at_once * i + k)
             return 0
 
-        if out_groups == at_once:
-            level_groups(0, 0)
-        else:
-            lax.fori_loop(0, out_groups // at_once, level_groups, 0)
+        lax.fori_loop(0, groups // at_once, level_pairs, 0)
 
     pl.semaphore_wait(barrier, devices + beams - 2)
     tiles = win[levels]
     per = rows // 8
     dests = 8 // per
 
+    early = win[levels - 3] - tiles
+    sublane = lax.broadcasted_iota(jnp.int32, (8, LANES), 0)
+
     def last_levels(q):
-        nodes = [
-            [
-                [turn_ref[w, pl.ds(pl.multiple_of(64 * q, 64) + n, 8, stride=8), :]
-                    for w in range(tiles)
-                ]
-            ]
-            for n in range(8)
-        ]
+        nodes = []
+        for r in range(8):
+            base = 8 * r * q
+            whole, short = base // LANES, base % LANES
+
+            def tile(w):
+                at = jnp.maximum(w + early - whole, 0)
+                x = turn_ref[at, pl.ds(pl.multiple_of(64 * q, 64) + r, 8, stride=8), :]
+                return x if r == 0 else pltpu.roll(x, short, 1)
+
+            if r == 0:
+                nodes.append([[tile(w) for w in range(tiles)]])
+                continue
+            moved = [tile(w) for w in range(-2, tiles)]
+            moved = [late_tiles(y, x, short) for x, y in zip(moved, moved[1:])]
+            moved = [pltpu.roll(x, 0, 1, stride=r, stride_axis=0) for x in moved]
+            nodes.append(
+                [[late_tiles(y, x, r * sublane) for x, y in zip(moved, moved[1:])]]
+            )
         for s in range(3):
             merged = []
             for j in range(len(nodes) // 2):
@@ -332,15 +349,20 @@
         )
 
     chunks = chan // 64
-    own = me // dests
-    for i in range(1, chunks):
-        q = lax.rem(own + i, chunks)
+
+    def chunk(i, _):
+        q = lax.rem(me // dests + i, chunks)
         last_levels(q)
         for h in range(dests):
-            exchange(dests * q + h, me).start()
-    last_levels(own)
-    for h in range(1, dests):
-        exchange(dests * own + lax.rem(me + h, dests), me).start()
+            target = dests * q + h
+
+            @pl.when(target != me)
+            def _():
+                exchange(target, me).start()
+
+        return 0
+
+    lax.fori_loop(1, chunks + 1, chunk, 0)
     recv_ref[me] = send_ref[me]
     for o in range(1, devices):
         other = lax.rem(me + o, devices)
@@ -355,7 +377,7 @@
         roots = jnp.where(lane == i, jnp.sqrt(jnp.float32(2**i)), roots)
     samples = block_tiles * LANES
 
-    def finish(m):
+    def finish(m, _):
         nodes = [
             [
                 [recv_ref[j, w, pl.ds(pl.multiple_of(8 * m, 8), 8), :] for w in range(tiles)]
@@ -388,13 +410,9 @@
                 peaks = jnp.where(lane == i, jnp.max(top, axis=1, keepdims=True), peaks)
             ratio = (peaks - widths * average) / (roots * deviation)
             snr_ref[pl.ds(8 * devices * m + c, 8, stride=devices), :] = ratio
-
-    def finish_both(i, _):
-        finish(2 * i)
-        finish(2 * i + 1)
         return 0
 
-    lax.fori_loop(0, rows // 16, finish_both, 0)
+    lax.fori_loop(0, rows // 8, finish, 0)
 
     peak = snr_ref[...].T[:8]
     trial = me * chan + lax.broadcasted_iota(jnp.int32, (8, chan), 1)
@@ -427,22 +445,22 @@
     levels = chan.bit_length() - 1
     cross = devices.bit_length() - 1
     tail_tiles, block_tiles = tail_len // LANES, block_len // LANES
-    win = windows(levels + cross, block_len + 2 ** (WIDTHS - 1) - 1, tail_tiles + block_tiles)
+    win = windows(levels, devices, block_len + 2 ** (WIDTHS - 1) - 1)
     rows = chan // devices
-    scratch = [pltpu.VMEM((win[0], chan, LANES), jnp.float32)]
+    scratch = [pltpu.VMEM((win[0] + 1, chan, LANES), jnp.float32)]
     for s in range(1, levels - 3):
         scratch.append(
-            pltpu.VMEM((1 << (levels - 3 - s), 1 << s, win[s], 8, LANES), jnp.float32)
+            pltpu.VMEM((1 << (levels - 3 - s), 1 << s, win[s] + 1, 8, LANES), jnp.float32)
         )
     tiles = win[levels]
     scratch += [
-        pltpu.VMEM((tiles, chan, LANES), jnp.float32),
+        pltpu.VMEM((win[levels - 3], chan, LANES), jnp.float32),
         pltpu.VMEM((devices, tiles, rows, LANES), jnp.float32),
         pltpu.VMEM((devices, tiles, rows, LANES), jnp.float32),
         pltpu.VMEM((chan, LANES), jnp.float32),
         pltpu.VMEM((beams, 8, chan), jnp.float32),
         pltpu.VMEM((chan, tail_len + block_len), jnp.bfloat16),
-        pltpu.SemaphoreType.DMA((tail_len // PIECE + 1,)),
+        pltpu.SemaphoreType.DMA(((tail_len + block_len) // PIECE,)),
         pltpu.SemaphoreType.DMA((devices,)),
         pltpu.SemaphoreType.DMA((devices,)),
         pltpu.SemaphoreType.DMA((beams,)),
@@ -457,7 +475,7 @@
         out_specs=(pl.BlockSpec(memory_space=pltpu.VMEM),) * 2,
         scratch_shapes=scratch,
         compiler_params=pltpu.CompilerParams(
-            collective_id=0, has_side_effects=True, vmem_limit_bytes=48 * 2**20
+            collective_id=0, has_side_effects=True, vmem_limit_bytes=60 * 2**20
         ),
     )(tail_blocks, dm_limit, block_samples, tail_samples)
 

time: 40 us -> 34.2 us (0.86)
  Pallas kernels: 34.5 us -> 30.1 us
  local copies, waits for them, and re-layouts: 3.32 us -> 1.91 us
    pallas_call x1, Pallas kernels: 34.5 us -> 30.1 us  [fused_local(): pl.pallas_call(functools.partial(fused, levels, cross, devices, beams, wi...]
    unnamed x4 -> x2, local copies, waits for them, and re-layouts: 2.12 us -> 0.01 us
    pallas_call x2, local copies, waits for them, and re-layouts: 1.2 us -> 1.9 us  [fused_local(): pl.pallas_call(functools.partial(fused, levels, cross, devices, beams, wi...]
where the time goes in v3:
time: 34.2 us; the launch traced here: 34 us
  Pallas kernels  30.1 us (88%)
  between operations  1.94 us (6%)
  local copies, waits for them, and re-layouts  1.91 us (6%)
    pallas_call x1, Pallas kernels, fused_local(): pl.pallas_call(functools.partial(fused, levels, cross, devices, beams, wi...  30.1 us
    pallas_call x2, local copies, waits for them, and re-layouts, fused_local(): pl.pallas_call(functools.partial(fused, levels, cross, devices, beams, wi...  1.9 us

profile of v3, /device:TPU:0, one launch (start us, length us, event | category | flops | bytes accessed | tf_op | source)
XLA Modules:
  0.0 34.0 jit_solution(5873634694943574443)
XLA Ops:
  1.9 30.1 %shard_map.59 = (f32[1,7,256]{2,1,0:T(8,128)}, f32[1,7,256]{2,1,0:T(8,128)}) custom-call(s32[1]{0:T(128)S(6)} %copy.8.tb_ref, s32[1]{0:T(128)S(6)} %copy.9.lim_ref, bf16[1,256,256]{2,1,0:T(8,128)(2,1)} %block_ref.1, bf16[1,256,2048]{2,1,0:T(8,128)(2,1)} %tail_ref.1), custom_call_target="tpu_custom_call" | custom-call | tf_op jit(solution)/shard_map/pallas_call | solution.py:470
  32.1 0.0 copy-start
  32.1 1.3 %copy.6 = f32[1,7,256]{2,0,1:T(1,128)} copy(f32[1,7,256]{2,1,0:T(8,128)} %get-tuple-element.2) | data formatting | bytes 14336 | tf_op jit(solution)/shard_map/pallas_call | solution.py:470
  33.4 0.0 copy-done
  33.4 0.6 %copy.7 = f32[1,7,256]{2,0,1:T(1,128)} copy(f32[1,7,256]{2,1,0:T(8,128)S(1)} %copy-done) | data formatting | bytes 14336 | tf_op jit(solution)/shard_map/pallas_call | solution.py:470
Async XLA Ops:
  32.1 1.3 %copy-start = (f32[1,7,256]{2,1,0:T(8,128)S(1)}, f32[1,7,256]{2,1,0:T(8,128)}, u32[]{:S(2)}) copy-start(f32[1,7,256]{2,1,0:T(8,128)} %get-tuple-element.3) | copy-start | bytes 21508

commit v4 on v3

--- a/solution.py
+++ b/solution.py
@@ -125,7 +125,7 @@
 LANES = 128
 PIECE = 256
 SPLITS = 3
-AT_ONCE = (2, 4, 4, 4, 4)
+AT_ONCE = (2, 2, 4, 4, 4)
 MESH_ID = pl.DeviceIdType.MESH
 
 
@@ -229,15 +229,21 @@
     def split(i, _):
         for k in range(SPLITS):
             at = pl.multiple_of((SPLITS * i + k) * PIECE, PIECE)
-            piece = held_ref.at[:, pl.ds(at, PIECE)]
             pltpu.make_async_copy(
-                block_ref.at[0, :, :PIECE], piece, load_sem.at[SPLITS * i + k]
+                block_ref.at[0, :, :PIECE],
+                held_ref.at[:, pl.ds(at, PIECE)],
+                load_sem.at[SPLITS * i + k],
             ).wait()
-            part = jnp.dot(pick, piece[...], preferred_element_type=jnp.float32)
-            for h in range(PIECE // LANES):
-                tile = (SPLITS * i + k) * (PIECE // LANES) + h
-                gain = jnp.where(tile >= first_valid, 1.0, 0.0).astype(jnp.float32)
-                split_ref[fill + tile] = part[:, LANES * h : LANES * (h + 1)] * gain
+        wide = SPLITS * PIECE
+        part = jnp.dot(
+            pick,
+            held_ref[:, pl.ds(pl.multiple_of(wide * i, wide), wide)],
+            preferred_element_type=jnp.float32,
+        )
+        for h in range(wide // LANES):
+            tile = i * (wide // LANES) + h
+            gain = jnp.where(tile >= first_valid, 1.0, 0.0).astype(jnp.float32)
+            split_ref[fill + tile] = part[:, LANES * h : LANES * (h + 1)] * gain
         return 0
 
     lax.fori_loop(0, len(pieces) // SPLITS, split, 0)
@@ -275,6 +281,9 @@
             odd = late_tiles(first[1:], first[:-1], short) + late_tiles(
                 second[1:], second[:-1], short + 1
             )
+            return g, e, even, odd
+
+        def keep_pair(g, e, even, odd, s=s):
             if s + 1 < levels - 3:
                 target = stage_refs[s]
                 target[g, 2 * e, 1:] = even
@@ -286,9 +295,10 @@
 
         at_once = AT_ONCE[min(s, len(AT_ONCE) - 1)]
 
-        def level_pairs(i, _, level_pair=level_pair, at_once=at_once):
-            for k in range(at_once):
-                level_pair(at_once * i + k)
+        def level_pairs(i, _, level_pair=level_pair, keep_pair=keep_pair, at_once=at_once):
+            pairs = [level_pair(at_once * i + k) for k in range(at_once)]
+            for pair in pairs:
+                keep_pair(*pair)
             return 0
 
         lax.fori_loop(0, groups // at_once, level_pairs, 0)

time: 34.2 us -> 33.6 us (0.982)
  Pallas kernels: 30.1 us -> 29.6 us
    pallas_call x1, Pallas kernels: 30.1 us -> 29.6 us  [fused_local(): pl.pallas_call(functools.partial(fused, levels, cross, devices, beams, wi...]
where the time goes in v4:
time: 33.6 us; the launch traced here: 33.4 us
  Pallas kernels  29.6 us (88%)
  between operations  1.94 us (6%)
  local copies, waits for them, and re-layouts  1.91 us (6%)
    pallas_call x1, Pallas kernels, fused_local(): pl.pallas_call(functools.partial(fused, levels, cross, devices, beams, wi...  29.6 us
    pallas_call x2, local copies, waits for them, and re-layouts, fused_local(): pl.pallas_call(functools.partial(fused, levels, cross, devices, beams, wi...  1.9 us

profile of v4, /device:TPU:0, one launch (start us, length us, event | category | flops | bytes accessed | tf_op | source)
XLA Modules:
  0.0 33.4 jit_solution(16286484251613450490)
XLA Ops:
  1.9 29.6 %shard_map.59 = (f32[1,7,256]{2,1,0:T(8,128)}, f32[1,7,256]{2,1,0:T(8,128)}) custom-call(s32[1]{0:T(128)S(6)} %copy.8.tb_ref, s32[1]{0:T(128)S(6)} %copy.9.lim_ref, bf16[1,256,256]{2,1,0:T(8,128)(2,1)} %block_ref.1, bf16[1,256,2048]{2,1,0:T(8,128)(2,1)} %tail_ref.1), custom_call_target="tpu_custom_call" | custom-call | tf_op jit(solution)/shard_map/pallas_call | solution.py:480
  31.5 0.0 copy-start
  31.5 1.3 %copy.6 = f32[1,7,256]{2,0,1:T(1,128)} copy(f32[1,7,256]{2,1,0:T(8,128)} %get-tuple-element.2) | data formatting | bytes 14336 | tf_op jit(solution)/shard_map/pallas_call | solution.py:480
  32.8 0.0 copy-done
  32.8 0.6 %copy.7 = f32[1,7,256]{2,0,1:T(1,128)} copy(f32[1,7,256]{2,1,0:T(8,128)S(1)} %copy-done) | data formatting | bytes 14336 | tf_op jit(solution)/shard_map/pallas_call | solution.py:480
Async XLA Ops:
  31.5 1.3 %copy-start = (f32[1,7,256]{2,1,0:T(8,128)S(1)}, f32[1,7,256]{2,1,0:T(8,128)}, u32[]{:S(2)}) copy-start(f32[1,7,256]{2,1,0:T(8,128)} %get-tuple-element.3) | copy-start | bytes 21508

commit v5 on v4

--- a/solution.py
+++ b/solution.py
@@ -182,8 +182,7 @@
     lim_ref,
     block_ref,
     tail_ref,
-    peak_ref,
-    excess_ref,
+    out_ref,
     split_ref,
     *rest,
 ):
@@ -251,14 +250,16 @@
     for ref in stage_refs:
         ref[:, :, 0] = jnp.zeros((ref.shape[0], ref.shape[1], 8, LANES), jnp.float32)
     lane_row = lax.broadcasted_iota(jnp.int32, (8, LANES), 1)
+    later_levels = []
     for s in range(levels - 3):
         out_groups = 1 << (levels - 4 - s)
         out_tiles = win[s + 1]
         unit = 1 << (levels - 1 - s)
         trials = 1 << s
 
-        def level_pair(index, s=s, out_tiles=out_tiles, unit=unit, trials=trials):
-            g, e = index // trials, index % trials
+        def level_pair(index, part, s=s, out_tiles=out_tiles, unit=unit, trials=trials):
+            count = max(trials // 2, 1)
+            g, e = index // count, part * count + index % count
             if s == 0:
                 held_tiles = split_ref.shape[0]
 
@@ -295,15 +296,17 @@
 
         at_once = AT_ONCE[min(s, len(AT_ONCE) - 1)]
 
-        def level_pairs(i, _, level_pair=level_pair, keep_pair=keep_pair, at_once=at_once):
-            pairs = [level_pair(at_once * i + k) for k in range(at_once)]
-            for pair in pairs:
-                keep_pair(*pair)
-            return 0
-
-        lax.fori_loop(0, groups // at_once, level_pairs, 0)
-
-    pl.semaphore_wait(barrier, devices + beams - 2)
+        def level(part, s=s, level_pair=level_pair, keep_pair=keep_pair, at_once=at_once):
+            def level_pairs(i, _):
+                pairs = [level_pair(at_once * i + k, part) for k in range(at_once)]
+                for pair in pairs:
+                    keep_pair(*pair)
+                return 0
+
+            lax.fori_loop(0, (groups if s == 0 else groups // 2) // at_once, level_pairs, 0)
+
+        later_levels.append(level)
+
     tiles = win[levels]
     per = rows // 8
     dests = 8 // per
@@ -360,19 +363,32 @@
 
     chunks = chan // 64
 
-    def chunk(i, _):
-        q = lax.rem(me // dests + i, chunks)
-        last_levels(q)
-        for h in range(dests):
-            target = dests * q + h
-
-            @pl.when(target != me)
-            def _():
-                exchange(target, me).start()
-
+    own = me // dests
+    chunks_part = chunks // 2
+
+    def half_of_trials(turn, _):
+        part = lax.rem(own // chunks_part + 1 + turn, 2)
+        for level in later_levels[1:]:
+            level(part)
+
+        def chunk(i, _):
+            q = part * chunks_part + lax.rem(own % chunks_part + 1 + i, chunks_part)
+            last_levels(q)
+            for h in range(dests):
+                target = dests * q + h
+
+                @pl.when(target != me)
+                def _():
+                    exchange(target, me).start()
+
+            return 0
+
+        lax.fori_loop(0, chunks_part, chunk, 0)
         return 0
 
-    lax.fori_loop(1, chunks + 1, chunk, 0)
+    later_levels[0](0)
+    pl.semaphore_wait(barrier, devices + beams - 2)
+    lax.fori_loop(0, 2, half_of_trials, 0)
     recv_ref[me] = send_ref[me]
     for o in range(1, devices):
         other = lax.rem(me + o, devices)
@@ -440,13 +456,16 @@
         )
         copy.start()
         copies.append(copy)
-    peak_ref[0] = peak[:WIDTHS]
+    for i in range(8):
+        out_ref[i] = peak[i : i + 1]
     for copy in copies:
         copy.wait()
     total = beam_ref[0]
     for b in range(1, beams):
         total = total + beam_ref[b]
-    excess_ref[0] = (peak - total / beams)[:WIDTHS]
+    mean = total / beams
+    for i in range(8):
+        out_ref[8 + i] = mean[i : i + 1]
 
 
 def fused_local(devices, beams, block_samples, tail_samples, tail_blocks, dm_limit):
@@ -476,22 +495,23 @@
         pltpu.SemaphoreType.DMA((beams,)),
         pltpu.SemaphoreType.DMA((beams,)),
     ]
-    out = jax.ShapeDtypeStruct((1, WIDTHS, chan), jnp.float32)
-    return pl.pallas_call(
+    both = pl.pallas_call(
         functools.partial(fused, levels, cross, devices, beams, win, tail_tiles, block_tiles),
-        out_shape=(out, out),
+        out_shape=jax.ShapeDtypeStruct((16, 1, chan), jnp.float32),
         in_specs=[pl.BlockSpec(memory_space=pltpu.SMEM)] * 2
         + [pl.BlockSpec(memory_space=pltpu.HBM)] * 2,
-        out_specs=(pl.BlockSpec(memory_space=pltpu.VMEM),) * 2,
+        out_specs=pl.BlockSpec(memory_space=pltpu.VMEM),
         scratch_shapes=scratch,
         compiler_params=pltpu.CompilerParams(
             collective_id=0, has_side_effects=True, vmem_limit_bytes=60 * 2**20
         ),
     )(tail_blocks, dm_limit, block_samples, tail_samples)
+    peak, mean = both[:WIDTHS], both[8 : 8 + WIDTHS]
+    return jnp.transpose(peak, (1, 0, 2)), jnp.transpose(peak - mean, (1, 0, 2))
 
 
 def fits(devices, beams_all, beams, chan):
-    return beams_all == beams and chan % (16 * devices) == 0 and chan <= 64 * devices and chan >= 64
+    return beams_all == beams and chan % (16 * devices) == 0 and chan <= 64 * devices and chan >= 128
 
 
 def solution(mesh):

time: 33.6 us -> 31.7 us (0.943)
  local copies, waits for them, and re-layouts: 1.91 us -> 0 us
  other arithmetic: 0 us -> 1.32 us
  Pallas kernels: 29.6 us -> 28.3 us
    pallas_call x2 -> x0, local copies, waits for them, and re-layouts: 1.9 us -> none  [fused_local(): pl.pallas_call(functools.partial(fused, levels, cross, devices, beams, wi...]
    transpose x0 -> x1, other arithmetic: none -> 1.32 us  [fused_local(): jnp.transpose(peak - mean, (1, 0, 2))]
    pallas_call x1, Pallas kernels: 29.6 us -> 28.3 us  [fused_local(): pl.pallas_call(functools.partial(fused, levels, cross, devices, beams, wi...]
where the time goes in v5:
time: 31.7 us; the launch traced here: 31.5 us
  Pallas kernels  28.3 us (89%)
  between operations  1.93 us (6%)
  other arithmetic  1.32 us (4%)
    pallas_call x1, Pallas kernels, fused_local(): pl.pallas_call(functools.partial(fused, levels, cross, devices, beams, wi...  28.3 us
    transpose x1, other arithmetic, fused_local(): jnp.transpose(peak - mean, (1, 0, 2))  1.32 us

profile of v5, /device:TPU:0, one launch (start us, length us, event | category | flops | bytes accessed | tf_op | source)
XLA Modules:
  0.0 31.5 jit_solution(5851939626992407232)
XLA Ops:
  1.9 28.3 %shard_map.59 = f32[16,1,256]{2,1,0:T(1,128)} custom-call(s32[1]{0:T(128)S(6)} %copy.6.tb_ref, s32[1]{0:T(128)S(6)} %copy.7.lim_ref, bf16[1,256,256]{2,1,0:T(8,128)(2,1)} %block_ref.1, bf16[1,256,2048]{2,1,0:T(8,128)(2,1)} %tail_ref.1), custom_call_target="tpu_custom_call" | custom-call | tf_op jit(solution)/shard_map/pallas_call | solution.py:498
  30.2 1.3 %subtract_bitcast_fusion = (f32[1,7,256]{2,0,1:T(1,128)}, f32[1,7,256]{2,0,1:T(1,128)}) fusion(f32[16,1,256]{2,1,0:T(1,128)} %shard_map.59), kind=kLoop, calls=%fused_computation | loop fusion | flops 1792 | bytes 28672 | tf_op jit(solution)/shard_map/transpose | solution.py:510
